TPU v7x, 128 devices: a whole 4x4x4 slice. The times are simulated.
128 devices in a mesh: grp: 8 (over x, y_hi), in: 16 (over y_lo, z, core).
Axes of the slice: x: 4, y: 4 (y_hi: 2, y_lo: 2; y = y_hi * 2 + y_lo), z: 4, core: 2. Of those that a mesh axis runs over, the one named last changes fastest.
Arguments:
- view_one: float32 [32768, 256], P(('grp', 'in')), may hold values from -6 to 6
- view_two: float32 [32768, 256], P(('grp', 'in')), may hold values from -6 to 6
Outputs:
- loss: float32 [], replicated
- grad_one: float32 [32768, 256], P(('grp', 'in'))
- grad_two: float32 [32768, 256], P(('grp', 'in'))
All inputs are finite; a program needn't handle non-finite values.
Results may differ from a plain program's by a relative error of at most 0.005.
Values may be sent and summed in bfloat16 or wider, within the bound.
A program may use at most 192 MiB of HBM per device.

v0:
```python
import jax
import jax.numpy as jnp
from jax import lax
from jax.sharding import PartitionSpec as P

logit_sharpness = 0.2


def summation_axes(first, second):
    return lax.dot_general(
        first, second, (((1,), (1,)), ((), ())), preferred_element_type=jnp.float32
    )


def shards(view_one, view_two):
    local_rows = view_one.shape[0]
    all_rows = local_rows * lax.axis_size("grp") * lax.axis_size("in")
    norm_one = jnp.sqrt(jnp.sum(view_one * view_one, axis=1, keepdims=True))
    unit_one = view_one / norm_one
    norm_two = jnp.sqrt(jnp.sum(view_two * view_two, axis=1, keepdims=True))
    unit_two = view_two / norm_two
    source_unit_vectors = unit_one.astype(jnp.bfloat16)
    target_unit_vectors = unit_two.astype(jnp.bfloat16)
    group_right = lax.all_gather(target_unit_vectors, "in", axis=0, tiled=True)
    shard_entry_count = lax.all_gather(group_right, "grp", axis=0, tiled=True)
    cosine_logit_matrix = summation_axes(source_unit_vectors, shard_entry_count) / logit_sharpness
    weights = jnp.exp(cosine_logit_matrix)
    partition_function_sums = jnp.sum(weights, axis=1)
    matched_exp_terms = jnp.dot(
        weights.astype(jnp.bfloat16), shard_entry_count, preferred_element_type=jnp.float32
    )
    partition_function_sums, matched_exp_terms = (partition_function_sums, matched_exp_terms)
    matched_pair_logits = (
        jnp.sum(
            source_unit_vectors.astype(jnp.float32) * target_unit_vectors.astype(jnp.float32),
            axis=1,
        )
        / logit_sharpness
    )
    loss_part = jnp.sum(jnp.log(partition_function_sums) - matched_pair_logits)
    loss = lax.psum(loss_part, ("grp", "in")) / all_rows
    logit_scale_factor = 1.0 / partition_function_sums
    denominator_flip = logit_scale_factor.astype(jnp.bfloat16)
    group_left, group_recip = (
        lax.all_gather(source_unit_vectors, "in", axis=0, tiled=True),
        lax.all_gather(denominator_flip, "in", axis=0, tiled=True),
    )
    source_shard_matrix = lax.all_gather(group_left, "grp", axis=0, tiled=True)
    shard_recip = lax.all_gather(group_recip, "grp", axis=0, tiled=True)
    cosine_logit_matrix = summation_axes(target_unit_vectors, source_shard_matrix) / logit_sharpness
    weights = (jnp.exp(cosine_logit_matrix) * shard_recip.astype(jnp.float32)[None, :]).astype(
        jnp.bfloat16
    )
    target_slot = jnp.dot(weights, source_shard_matrix, preferred_element_type=jnp.float32)
    source_embedding_grad = (
        matched_exp_terms * logit_scale_factor[:, None] - target_unit_vectors.astype(jnp.float32)
    ) / logit_sharpness
    target_embedding_grad = (
        target_slot - source_unit_vectors.astype(jnp.float32)
    ) / logit_sharpness
    grad_one = (
        source_embedding_grad
        - unit_one * jnp.sum(unit_one * source_embedding_grad, axis=1, keepdims=True)
    ) / norm_one
    grad_two = (
        target_embedding_grad
        - unit_two * jnp.sum(unit_two * target_embedding_grad, axis=1, keepdims=True)
    ) / norm_two
    return (loss, grad_one, grad_two)


def solution(mesh):
    return jax.shard_map(
        shards,
        mesh=mesh,
        in_specs=(P(("grp", "in"), None), P(("grp", "in"), None)),
        out_specs=(P(), P(("grp", "in"), None), P(("grp", "in"), None)),
        check_vma=False,
    )
```

profile of v0, /device:TPU:1, one launch (start us, length us, event | category | flops | bytes accessed | tf_op | source)
XLA Modules:
  0.0 533.0 jit_solution(7902696129782554760)
XLA Ops:
  7.2 0.0 all-gather.6.cloned.1.call-start
  7.2 1.1 copy.13
  8.3 1.1 multiply_reduce_fusion.3
  9.4 1.1 copy.14
  10.5 1.1 multiply_reduce_fusion.2
  11.5 0.8 fusion.18
  12.3 0.0 all-gather.6.cloned.1.call-update
  12.3 0.0 all-gather.10.cloned.1.call-start
  12.4 0.7 all-gather.10.cloned.1.call-update
  13.1 0.0 all-gather.8.cloned.1.call-start
  13.1 40.4 %all-gather.6.cloned.1.call-done = bf16[4096,256]{0,1:T(8,128)(2,1)} async-done(((bf16[256,256]{0,1:T(8,128)(2,1)}), bf16[4096,256]{0,1:T(8,128)(2,1)}) %all-gather.6.cloned.1.call-update) | async-done | bytes 2097168 | tf_op jit(solution)/shard_map/all_gather | solution.py:24
  53.5 0.0 all-gather.8.cloned.1.call-update
  53.5 0.0 all-gather.12.cloned.1.call-start
  53.6 39.7 %all-gather.10.cloned.1.call-done = bf16[4096,256]{0,1:T(8,128)(2,1)} async-done(((bf16[256,256]{0,1:T(8,128)(2,1)}), bf16[4096,256]{0,1:T(8,128)(2,1)}) %all-gather.10.cloned.1.call-update) | async-done | bytes 2097168 | tf_op jit(solution)/shard_map/all_gather | solution.py:45
  93.3 0.0 all-gather.12.cloned.1.call-update
  93.3 0.0 copy-start.1
  93.3 187.6 %all-gather.8.cloned.1.call-done = bf16[32768,256]{0,1:T(8,128)(2,1)} async-done(((bf16[4096,256]{0,1:T(8,128)(2,1)}), bf16[32768,256]{0,1:T(8,128)(2,1)}) %all-gather.8.cloned.1.call-update) | async-done | bytes 16777232 | tf_op jit(solution)/shard_map/all_gather | solution.py:25
  280.9 15.1 %fusion.25 = (f32[256]{0:T(256)S(1)}, bf16[256,32768]{1,0:T(8,128)(2,1)}) fusion(bf16[256,256]{0,1:T(8,128)(2,1)} %get-tuple-element.15, bf16[32768,256]{0,1:T(8,128)(2,1)} %all-gather.8.cloned.1.call-done), kind=kOutput, calls=%fused_computation.30 | convolution fusion | flops 4320133120 | bytes 33686528 | tf_op jit(solution)/shard_map/dot_general | solution.py:10
  296.0 0.6 fusion.22
  296.6 143.8 %psum.7 = f32[]{:T(128)} all-reduce(f32[]{:T(128)} %get-tuple-element.17), channel_id=1, replica_groups=mesh['grp'=8,'in'=16] {'grp','in'}, use_global_device_ids=true, to_apply=%region_5.0 | all-reduce | flops 1 | bytes 8 | tf_op jit(solution)/shard_map/psum | solution.py:41
  440.4 0.0 copy-done.1
  440.4 0.0 copy-start
  440.4 19.8 %multiply_reduce_fusion.1 = (f32[256]{0:T(256)S(1)}, f32[256,256]{0,1:T(8,128)S(1)}) fusion(f32[256,256]{0,1:T(8,128)S(1)} %copy.13, f32[256]{0:T(256)S(1)} %sqrt.16, bf16[256,256]{0,1:T(8,128)(2,1)S(1)} %copy-done.1, f32[256]{0:T(256)S(1)} %get-tuple-element.13, bf16[32768,256]{0,1:T(8,128)(2,1)} %all-gather.8.cloned.1.call-done, ...), kind=kOutput, calls=%fused_computation.19 | convolution fusion | flops 4295426048 | bytes 34212864 | tf_op jit(solution)/shard_map/dot_general | solution.py:29
  460.2 0.8 copy.15
  461.1 19.4 %all-gather = bf16[16,1,256]{2,1,0:T(2,128)(2,1)S(1)} all-gather(bf16[1,1,256]{2,1,0:T(2,128)(2,1)S(1)} %reshape.20), channel_id=1, replica_groups=mesh['grp'=8,'in'=16] {'in'}, dimensions={0}, use_global_device_ids=true | all-gather | bytes 8704 | tf_op jit(solution)/shard_map/all_gather | solution.py:46
  480.5 28.0 %all_gather.23 = bf16[32768]{0:T(1024)(128)(2,1)S(1)} all-gather(bf16[4096]{0:T(1024)(128)(2,1)S(1)} %bitcast.10), channel_id=1, replica_groups=mesh['grp'=8,'in'=16] {'grp'}, dimensions={0}, use_global_device_ids=true | all-gather | bytes 73728 | tf_op jit(solution)/shard_map/all_gather | solution.py:49
  508.5 0.0 all-gather.12.cloned.1.call-done
  508.6 0.0 copy-done
  508.6 15.2 %multiply_reduce_fusion = (f32[256]{0:T(256)S(1)}, f32[256,256]{0,1:T(8,128)S(1)}) fusion(f32[256,256]{0,1:T(8,128)S(1)} %copy.14, f32[256]{0:T(256)S(1)} %sqrt.17, bf16[256,256]{0,1:T(8,128)(2,1)S(1)} %copy-done, bf16[32768,256]{0,1:T(8,128)(2,1)} %all-gather.12.cloned.1.call-done, bf16[256,256]{0,1:T(8,128)(2,1)S(1)} %copy-done.1, ...), kind=kOutput, calls=%fused_computation.17 | convolution fusion | flops 8615493632 | bytes 17696768 | tf_op jit(solution)/shard_map/dot_general | solution.py:54
  523.9 0.8 copy.16
  (8 shorter events, 0.2 us)
Async XLA Ops:
  7.2 46.3 %all-gather.6.cloned.1.call-start = ((), (), s32[]{:S(2)}) async-start(), calls=%async_computation | async-start | bytes 2228224 | tf_op jit(solution)/shard_map/all_gather | solution.py:24
  12.3 80.9 %all-gather.10.cloned.1.call-start = ((), (), s32[]{:S(2)}) async-start(), calls=%async_computation.2 | async-start | bytes 2228224 | tf_op jit(solution)/shard_map/all_gather | solution.py:45
  13.1 267.8 %all-gather.8.cloned.1.call-start = ((), (), s32[]{:S(2)}) async-start(), calls=%async_computation.1 | async-start | bytes 18874368 | tf_op jit(solution)/shard_map/all_gather | solution.py:25
  53.5 455.1 %all-gather.12.cloned.1.call-start = ((), (), s32[]{:S(2)}) async-start(), calls=%async_computation.3 | async-start | bytes 18874368 | tf_op jit(solution)/shard_map/all_gather | solution.py:48
  93.3 347.1 %copy-start.1 = (bf16[256,256]{0,1:T(8,128)(2,1)S(1)}, bf16[256,256]{0,1:T(8,128)(2,1)}, u32[]{:S(2)}) copy-start(bf16[256,256]{0,1:T(8,128)(2,1)} %get-tuple-element.16) | copy-start | bytes 393220
  440.4 68.2 %copy-start = (bf16[256,256]{0,1:T(8,128)(2,1)S(1)}, bf16[256,256]{0,1:T(8,128)(2,1)}, u32[]{:S(2)}) copy-start(bf16[256,256]{0,1:T(8,128)(2,1)} %get-tuple-element.15) | copy-start | bytes 393220
Sparse Core Ops, SparseCore 0:
  12.4 40.9 all-gather.5
  55.7 37.5 all-gather.9
  95.6 185.2 all-gather.7
  283.1 185.3 all-gather.11
where the time goes:
time: 538 us; the launch traced here: 533 us
  waiting for transfers between devices  268 us (50%)
  blocking collectives  191 us (36%)
  matrix products  50.1 us (9%)
  between operations  15.6 us (3%)
    all_gather x1, waiting for transfers between devices, shards(): shard_entry_count = lax.all_gather(group_right, 'grp', axis=0, tiled=True)  188 us
    psum x1, blocking collectives, shards(): loss = lax.psum(loss_part, ('grp', 'in')) / all_rows  144 us
    all_gather x1, waiting for transfers between devices, shards(): group_right = lax.all_gather(target_unit_vectors, 'in', axis=0, tiled=True)  40.4 us
    all_gather x1, waiting for transfers between devices, shards(): lax.all_gather(source_unit_vectors, 'in', axis=0, tiled=True)  39.7 us
    all_gather x1, blocking collectives, shards(): shard_recip = lax.all_gather(group_recip, 'grp', axis=0, tiled=True)  28 us
    dot_general x1, matrix products, shards(): jnp.dot(weights.astype(jnp.bfloat16), shard_entry_count, preferred_elemen...  19.8 us
    all_gather x1, blocking collectives, shards(): lax.all_gather(denominator_flip, 'in', axis=0, tiled=True)  19.4 us
    dot_general x1, matrix products, shards(): jnp.dot(weights, source_shard_matrix, preferred_element_type=jnp.float32)  15.2 us
  transfers between devices with their start and end apart: 4, of which 3 were waited for; matrix products, arithmetic and copies ran while one was open for 7% of the time, Pallas kernels for 0%

commit v1 on v0

v1 whole, which is shorter than its diff:
```python
import functools

import jax
import jax.numpy as jnp
from jax import lax
from jax.experimental import pallas as pl
from jax.experimental.pallas import tpu as pltpu
from jax.sharding import PartitionSpec as P

MESH = pl.DeviceIdType.MESH
F32, BF16 = jnp.float32, jnp.bfloat16
SHARP = 5.0
EXP2_SCALE = 5.0 * 1.4426950408889634
B = 256
ORDER = (0, 4, 2, 1, 6, 3, 5, 7)
PLACE = {k: p for p, k in enumerate(ORDER)}
FAR = (7, 3, 5, 6, 4, 2, 1)
NEAR = (4, 2, 1)
HOP2 = ((2, 4), (1, 2), (4, 1))
HOP3 = ((3, 4, 0, 96), (5, 2, 96, 80), (6, 1, 176, 80))
A, BB = 0, 1


def position():
    g, i = lax.axis_index("grp"), lax.axis_index("in")
    return g // 2, 2 * (g % 2) + i // 8, (i // 2) % 4, i % 2


def flip_a(v):
    return v + 1 - 2 * (v % 2)


def flip_b(v):
    return (v + 3 + 2 * (v % 2)) % 4


def peer(group, k):
    x, y, z, c = position()
    flip = flip_b if group else flip_a
    x = flip(x) if k & 4 else x
    y = flip(y) if k & 2 else y
    z = flip(z) if k & 1 else z
    return (2 * x + y // 2, 8 * (y % 2) + 2 * z + c)


def sibling():
    return (lax.axis_index("grp"), flip_a(lax.axis_index("in")))


def rows(p, n=1):
    return pl.ds(p * B, n * B)


def nt(a, b):
    return lax.dot_general(a, b, (((1,), (1,)), ((), ())), preferred_element_type=F32)


def tn(a, b):
    return lax.dot_general(a, b, (((0,), (0,)), ((), ())), preferred_element_type=F32)


def nn(a, b):
    return lax.dot_general(a, b, (((1,), (0,)), ((), ())), preferred_element_type=F32)


def tree(parts):
    for bit in (1, 2, 4):
        parts = {k: parts[k] + parts[k ^ bit] for k in parts if not k & bit}
    return parts[0]


def kernel(
    one_ref, two_ref, loss_ref, g1_ref, g2_ref,
    left, right, weights, t8,
    tmine, tsib, tpair, tall,
    nsib_out, nsib_in, n_out, n_in, n_own,
    c_out, c_in, c_own,
    l_pair_out, l_pair_in, l_a_out, l_a_in, l_b_out, l_b_in,
    ss, rs,
):
    counter = [0]
    started = []

    def send(src, dst, device):
        n = counter[0]
        counter[0] += 1
        copy = pltpu.make_async_remote_copy(
            src_ref=src, dst_ref=dst, send_sem=ss.at[n], recv_sem=rs.at[n],
            device_id=device, device_id_type=MESH,
        )
        copy.start()
        started.append(copy)
        return copy

    barrier = pltpu.get_barrier_semaphore()
    pl.semaphore_signal(barrier, 1, device_id=sibling(), device_id_type=MESH)
    for k in FAR:
        for group in (A, BB):
            pl.semaphore_signal(barrier, 1, device_id=peer(group, k), device_id_type=MESH)

    one, two = one_ref[...], two_ref[...]
    norm_one = jnp.sqrt(jnp.sum(one * one, axis=1, keepdims=True))
    norm_two = jnp.sqrt(jnp.sum(two * two, axis=1, keepdims=True))
    left[rows(0), :] = (one / norm_one).astype(BF16)
    right[rows(0), :] = (two / norm_two).astype(BF16)
    pl.semaphore_wait(barrier, 15)

    bufs = (left, right)
    stride = (2, 1)

    def block(group, k, first=0, n=B):
        return bufs[group].at[pl.ds(stride[group] * PLACE[k] * B + first, n)]

    def to_sibling(k):
        return send(left.at[rows(2 * PLACE[k])], left.at[rows(2 * PLACE[k] + 1)], sibling())

    got, side = {}, {}
    for d in NEAR:
        for group in (BB, A):
            got[group, d] = send(block(group, 0), block(group, d), peer(group, d))
    side[0] = to_sibling(0)
    for frm, via in HOP2:
        for group in (BB, A):
            got[group, frm].wait_recv()
            got[group, frm | via] = send(block(group, frm), block(group, frm | via), peer(group, via))
        side[frm] = to_sibling(frm)

    def score(l0, l1, j0, j1):
        n = (j1 - j0) * B
        for lb in range(l0, l1):
            lanes = rows(lb)
            w = jnp.exp2(nt(right[rows(j0, j1 - j0), :], left[lanes, :]) * EXP2_SCALE)
            part = jnp.sum(w.reshape(n // 8, 8, B), axis=0)
            if j0 == 0:
                t8[:, lanes] = part
            else:
                t8[:, lanes] += part
            weights[rows(j0, j1 - j0), lanes] = w.astype(BF16)

    for k in (0, *NEAR):
        side[k].wait_recv()
    score(0, 8, 0, 4)
    last = {}
    for frm, via, first, n in HOP3:
        for group in (BB, A):
            got[group, frm].wait_recv()
            last[group, via] = send(block(group, frm, first, n), block(group, 7, first, n), peer(group, via))
        side[frm] = to_sibling(frm)
    for frm, *_ in HOP3:
        side[frm].wait_recv()
    score(8, 14, 0, 7)
    score(0, 8, 4, 7)
    for copy in last.values():
        copy.wait_recv()
    side[7] = to_sibling(7)
    score(0, 14, 7, 8)
    side[7].wait_recv()
    score(14, 16, 0, 8)

    tmine[...] = jnp.sum(t8[...], axis=0, keepdims=True)
    pair = send(tmine, tsib, sibling())

    def numer(p):
        return tn(weights[:, rows(p)], right[...])

    nsib = {}
    for n, k in enumerate((*FAR, 0)):
        nsib_out[PLACE[k]] = numer(2 * PLACE[k] + 1).astype(BF16)
        nsib[k] = send(nsib_out.at[PLACE[k]], nsib_in.at[PLACE[k]], sibling())
        if n == 0:
            pair.wait_recv()
            other = tsib[...]
            tpair[...] = tmine[...] + jnp.concatenate(
                [other[:, (p ^ 1) * B : (p ^ 1) * B + B] for p in range(16)], axis=1
            )
            tcopies = [send(tpair, tall.at[k], peer(A, k)) for k in FAR]
    ncopies = []
    for k in FAR:
        nsib[k].wait_recv()
        n_out[PLACE[k]] = (numer(2 * PLACE[k]) + nsib_in[PLACE[k]].astype(F32)).astype(BF16)
        ncopies.append(send(n_out.at[PLACE[k]], n_in.at[k], peer(A, k)))
    nsib[0].wait_recv()
    n_own[...] = numer(0) + nsib_in[0].astype(F32)
    for copy in tcopies:
        copy.wait_recv()

    def their_totals(k):
        if k == 0:
            return tpair[...]
        theirs = tall[k]
        places = [2 * PLACE[m ^ k] + c for m in ORDER for c in (0, 1)]
        return jnp.concatenate([theirs[:, p * B : p * B + B] for p in places], axis=1)

    totals = tree({k: their_totals(k) for k in range(8)})
    recip = 1.0 / totals
    recip_row = recip.astype(BF16)

    ccopies = []
    for k in FAR:
        part = nn(weights[rows(PLACE[k]), :] * recip_row, left[...])
        c_out[PLACE[k]] = part.astype(BF16)
        ccopies.append(send(c_out.at[PLACE[k]], c_in.at[k], peer(BB, k)))
    c_own[...] = nn(weights[rows(0), :] * recip_row, left[...])

    mine = jnp.sum(jnp.log(totals[:, :B]), axis=1, keepdims=True)
    unit_l, unit_r = left[rows(0), :].astype(F32), right[rows(0), :].astype(F32)
    dots = jnp.sum(jnp.sum(unit_l * unit_r, axis=1, keepdims=True), axis=0, keepdims=True)
    l_pair_out[...] = jnp.broadcast_to(mine - dots * SHARP, (8, 128))
    copy = send(l_pair_out, l_pair_in, sibling())
    copy.wait_recv()
    l_a_out[...] = l_pair_out[...] + l_pair_in[...]
    copies = [send(l_a_out, l_a_in.at[k], peer(A, k)) for k in FAR]
    for copy in copies:
        copy.wait_recv()
    l_b_out[...] = tree({k: l_a_in[k] if k else l_a_out[...] for k in range(8)})
    copies = [send(l_b_out, l_b_in.at[k], peer(BB, k)) for k in FAR]
    for copy in copies:
        copy.wait_recv()
    loss_ref[...] = tree({k: l_b_in[k] if k else l_b_out[...] for k in range(8)}) * (1.0 / (128 * B))

    def finish(x, grad, out):
        norm = jnp.sqrt(jnp.sum(x * x, axis=1, keepdims=True))
        unit = x / norm
        out[...] = (grad - unit * jnp.sum(unit * grad, axis=1, keepdims=True)) / norm

    scale = jnp.transpose(jnp.broadcast_to(recip[:, :B], (128, B)))
    scale = jnp.concatenate([scale, scale], axis=1)
    total = n_own[...]
    for copy, k in zip(ncopies, FAR):
        copy.wait_recv()
        total = total + n_in[k].astype(F32)
    finish(one_ref[...], (total * scale - right[rows(0), :].astype(F32)) * SHARP, g1_ref)
    total = c_own[...]
    for copy, k in zip(ccopies, FAR):
        copy.wait_recv()
        total = total + c_in[k].astype(F32)
    finish(two_ref[...], (total - left[rows(0), :].astype(F32)) * SHARP, g2_ref)
    for copy in started:
        copy.wait_send()


def step(one, two):
    vmem = pl.BlockSpec(memory_space=pltpu.VMEM)
    blocks = pltpu.VMEM((8, B, B), BF16)
    tile = pltpu.VMEM((8, 128), F32)
    tiles = pltpu.VMEM((8, 8, 128), F32)
    row = pltpu.VMEM((1, 16 * B), F32)
    copies = 2 * 9 + 8 + 8 + 15 + 7 + 15
    loss, g1, g2 = pl.pallas_call(
        kernel,
        out_shape=(
            jax.ShapeDtypeStruct((8, 128), F32),
            jax.ShapeDtypeStruct((B, B), F32),
            jax.ShapeDtypeStruct((B, B), F32),
        ),
        in_specs=[vmem] * 2,
        out_specs=(vmem,) * 3,
        scratch_shapes=[
            pltpu.VMEM((16 * B, B), BF16),
            pltpu.VMEM((8 * B, B), BF16),
            pltpu.VMEM((8 * B, 16 * B), BF16),
            pltpu.VMEM((8, 16 * B), F32),
            row, row, row, pltpu.VMEM((8, 1, 16 * B), F32),
            blocks, blocks, blocks, blocks, pltpu.VMEM((B, B), F32),
            blocks, blocks, pltpu.VMEM((B, B), F32),
            tile, tile, tile, tiles, tile, tiles,
            pltpu.SemaphoreType.DMA((copies,)),
            pltpu.SemaphoreType.DMA((copies,)),
        ],
        compiler_params=pltpu.CompilerParams(
            collective_id=1, has_side_effects=True, vmem_limit_bytes=56 * 2**20
        ),
    )(one, two)
    return loss[0, 0], g1, g2


def solution(mesh):
    return jax.shard_map(
        step,
        mesh=mesh,
        in_specs=(P(("grp", "in"), None), P(("grp", "in"), None)),
        out_specs=(P(), P(("grp", "in"), None), P(("grp", "in"), None)),
        check_vma=False,
    )
```

time: 538 us -> 63.1 us (0.12)
  waiting for transfers between devices: 268 us -> 0 us
  blocking collectives: 191 us -> 0 us
  Pallas kernels: 0 us -> 58.7 us
  matrix products: 50.1 us -> 0 us
  between operations: 15.6 us -> 0.64 us
    all_gather x4 -> x0, waiting for transfers between devices: 268 us -> none  [the longest x1 188 us: shards(): shard_entry_count = lax.all_gather(group_right, 'grp', axis=0, tiled=True)]
    psum x1 -> x0, blocking collectives: 144 us -> none  [shards(): loss = lax.psum(loss_part, ('grp', 'in')) / all_rows]
    pallas_call x0 -> x1, Pallas kernels: none -> 58.7 us  [step(): pl.pallas_call(kernel, out_shape=(jax.ShapeDtypeStruct((8, 128), F32), ja...]
    dot_general x3 -> x0, matrix products: 50.1 us -> none  [the longest x1 19.8 us: shards(): jnp.dot(weights.astype(jnp.bfloat16), shard_entry_count, preferred_elemen...]
    all_gather x2 -> x0, blocking collectives: 47.4 us -> none  [the longest x1 28 us: shards(): shard_recip = lax.all_gather(group_recip, 'grp', axis=0, tiled=True)]
  transfers between devices with their start and end apart: 4 -> 0, of which waited for: 3 -> 0; matrix products, arithmetic and copies ran while one was open for 7% -> 0% of each run, Pallas kernels for 0% -> 0%
where the time goes in v1:
time: 63.1 us; the launch traced here: 62.9 us
  Pallas kernels  58.7 us (93%)
  local copies, waits for them, and re-layouts  3.61 us (6%)
  between operations  0.64 us (1%)
    pallas_call x1, Pallas kernels, step(): pl.pallas_call(kernel, out_shape=(jax.ShapeDtypeStruct((8, 128), F32), ja...  58.7 us
    unnamed x4, local copies, waits for them, and re-layouts  2.42 us

profile of v1, /device:TPU:1, one launch (start us, length us, event | category | flops | bytes accessed | tf_op | source)
XLA Modules:
  0.0 62.9 jit_solution(11832871352622502299)
XLA Ops:
  0.6 58.7 %shard_map.49 = (f32[8,128]{1,0:T(8,128)}, f32[256,256]{1,0:T(8,128)}, f32[256,256]{1,0:T(8,128)}) custom-call(f32[256,256]{1,0:T(8,128)} %one_ref.1, f32[256,256]{1,0:T(8,128)} %two_ref.1), custom_call_target="tpu_custom_call" | custom-call | tf_op jit(solution)/shard_map/pallas_call | solution.py:249
  59.3 1.2 %slice.3 = f32[1,1]{1,0:T(1,128)} slice(f32[8,128]{1,0:T(8,128)} %get-tuple-element.6), slice={[0:1], [0:1]} | slice | bytes 8 | tf_op jit(solution)/shard_map/slice | solution.py:274
  60.5 0.0 copy-start
  60.5 1.7 %copy.7 = f32[256,256]{1,0:T(8,128)} copy(f32[256,256]{1,0:T(8,128)} %get-tuple-element.13) | data formatting | bytes 524288
  62.2 0.0 copy-done
  62.2 0.7 %copy.8 = f32[256,256]{1,0:T(8,128)} copy(f32[256,256]{1,0:T(8,128)S(1)} %copy-done) | data formatting | bytes 524288
Async XLA Ops:
  60.5 1.7 %copy-start = (f32[256,256]{1,0:T(8,128)S(1)}, f32[256,256]{1,0:T(8,128)}, u32[]{:S(2)}) copy-start(f32[256,256]{1,0:T(8,128)} %get-tuple-element.14) | copy-start | bytes 786436

commit v2 on v1

--- a/solution.py
+++ b/solution.py
@@ -94,7 +94,7 @@
 
     barrier = pltpu.get_barrier_semaphore()
     pl.semaphore_signal(barrier, 1, device_id=sibling(), device_id_type=MESH)
-    for k in FAR:
+    for k in NEAR:
         for group in (A, BB):
             pl.semaphore_signal(barrier, 1, device_id=peer(group, k), device_id_type=MESH)
 
@@ -103,7 +103,7 @@
     norm_two = jnp.sqrt(jnp.sum(two * two, axis=1, keepdims=True))
     left[rows(0), :] = (one / norm_one).astype(BF16)
     right[rows(0), :] = (two / norm_two).astype(BF16)
-    pl.semaphore_wait(barrier, 15)
+    pl.semaphore_wait(barrier, 7)
 
     bufs = (left, right)
     stride = (2, 1)
@@ -160,27 +160,51 @@
     tmine[...] = jnp.sum(t8[...], axis=0, keepdims=True)
     pair = send(tmine, tsib, sibling())
 
-    def numer(p):
-        return tn(weights[:, rows(p)], right[...])
-
-    nsib = {}
-    for n, k in enumerate((*FAR, 0)):
-        nsib_out[PLACE[k]] = numer(2 * PLACE[k] + 1).astype(BF16)
-        nsib[k] = send(nsib_out.at[PLACE[k]], nsib_in.at[PLACE[k]], sibling())
-        if n == 0:
-            pair.wait_recv()
-            other = tsib[...]
-            tpair[...] = tmine[...] + jnp.concatenate(
-                [other[:, (p ^ 1) * B : (p ^ 1) * B + B] for p in range(16)], axis=1
-            )
-            tcopies = [send(tpair, tall.at[k], peer(A, k)) for k in FAR]
-    ncopies = []
-    for k in FAR:
-        nsib[k].wait_recv()
-        n_out[PLACE[k]] = (numer(2 * PLACE[k]) + nsib_in[PLACE[k]].astype(F32)).astype(BF16)
-        ncopies.append(send(n_out.at[PLACE[k]], n_in.at[k], peer(A, k)))
-    nsib[0].wait_recv()
-    n_own[...] = numer(0) + nsib_in[0].astype(F32)
+    def numer(places, core):
+        return [tn(weights[:, rows(2 * p + core)], right[...]) for p in places]
+
+    def for_sibling(places):
+        for p, part in zip(places, numer(places, 1)):
+            nsib_out[p] = part.astype(BF16)
+        span = pl.ds(places[0], len(places))
+        return send(nsib_out.at[span], nsib_in.at[span], sibling())
+
+    def for_members(places, arrival):
+        parts = numer(places, 0)
+        arrival.wait_recv()
+        for p, part in zip(places, parts):
+            part = part + nsib_in[p].astype(F32)
+            if p == 0:
+                n_own[...] = part
+            else:
+                n_out[p] = part.astype(BF16)
+        for p in reversed(places):
+            if p:
+                ncopies[p] = send(n_out.at[p], n_in.at[ORDER[p]], peer(A, ORDER[p]))
+
+    def column(places):
+        span = rows(places[0], len(places))
+        part = nn(weights[span, :] * recip_row, left[...])
+        for n, p in enumerate(places):
+            if p == 0:
+                c_own[...] = part[:B]
+            else:
+                c_out[p] = part[n * B : n * B + B].astype(BF16)
+        for p in reversed(places):
+            if p:
+                ccopies[p] = send(c_out.at[p], c_in.at[ORDER[p]], peer(BB, ORDER[p]))
+
+    ncopies, ccopies = {}, {}
+    near, far = (0, 1, 2, 3), (4, 5, 6, 7)
+    far_sib = for_sibling(far)
+    pair.wait_recv()
+    other = tsib[...]
+    tpair[...] = tmine[...] + jnp.concatenate(
+        [other[:, (p ^ 1) * B : (p ^ 1) * B + B] for p in range(16)], axis=1
+    )
+    tcopies = [send(tpair, tall.at[k], peer(A, k)) for k in FAR]
+    near_sib = for_sibling(near)
+    for_members(far, far_sib)
     for copy in tcopies:
         copy.wait_recv()
 
@@ -195,12 +219,9 @@
     recip = 1.0 / totals
     recip_row = recip.astype(BF16)
 
-    ccopies = []
-    for k in FAR:
-        part = nn(weights[rows(PLACE[k]), :] * recip_row, left[...])
-        c_out[PLACE[k]] = part.astype(BF16)
-        ccopies.append(send(c_out.at[PLACE[k]], c_in.at[k], peer(BB, k)))
-    c_own[...] = nn(weights[rows(0), :] * recip_row, left[...])
+    column(far)
+    for_members(near, near_sib)
+    column(near)
 
     mine = jnp.sum(jnp.log(totals[:, :B]), axis=1, keepdims=True)
     unit_l, unit_r = left[rows(0), :].astype(F32), right[rows(0), :].astype(F32)
@@ -218,25 +239,28 @@
         copy.wait_recv()
     loss_ref[...] = tree({k: l_b_in[k] if k else l_b_out[...] for k in range(8)}) * (1.0 / (128 * B))
 
-    def finish(x, grad, out):
+    scale = jnp.transpose(jnp.broadcast_to(recip[:, :B], (128, B)))
+    scale = jnp.concatenate([scale, scale], axis=1)
+    total = n_own[...]
+    for p in reversed(range(1, 8)):
+        ncopies[p].wait_recv()
+        total = total + n_in[ORDER[p]].astype(F32)
+    g1_ref[...] = (total * scale - right[rows(0), :].astype(F32)) * SHARP
+    total = c_own[...]
+    for p in reversed(range(1, 8)):
+        ccopies[p].wait_recv()
+        total = total + c_in[ORDER[p]].astype(F32)
+    g2_ref[...] = (total - left[rows(0), :].astype(F32)) * SHARP
+    for copy in started:
+        copy.wait_send()
+
+
+def finish_kernel(one_ref, two_ref, loss_ref, g1_ref, g2_ref, out_loss, out_one, out_two):
+    for x, grad, out in ((one_ref[...], g1_ref[...], out_one), (two_ref[...], g2_ref[...], out_two)):
         norm = jnp.sqrt(jnp.sum(x * x, axis=1, keepdims=True))
         unit = x / norm
         out[...] = (grad - unit * jnp.sum(unit * grad, axis=1, keepdims=True)) / norm
-
-    scale = jnp.transpose(jnp.broadcast_to(recip[:, :B], (128, B)))
-    scale = jnp.concatenate([scale, scale], axis=1)
-    total = n_own[...]
-    for copy, k in zip(ncopies, FAR):
-        copy.wait_recv()
-        total = total + n_in[k].astype(F32)
-    finish(one_ref[...], (total * scale - right[rows(0), :].astype(F32)) * SHARP, g1_ref)
-    total = c_own[...]
-    for copy, k in zip(ccopies, FAR):
-        copy.wait_recv()
-        total = total + c_in[k].astype(F32)
-    finish(two_ref[...], (total - left[rows(0), :].astype(F32)) * SHARP, g2_ref)
-    for copy in started:
-        copy.wait_send()
+    out_loss[...] = loss_ref[0:1, 0:1]
 
 
 def step(one, two):
@@ -245,7 +269,7 @@
     tile = pltpu.VMEM((8, 128), F32)
     tiles = pltpu.VMEM((8, 8, 128), F32)
     row = pltpu.VMEM((1, 16 * B), F32)
-    copies = 2 * 9 + 8 + 8 + 15 + 7 + 15
+    copies = 2 * 9 + 8 + 8 + 2 + 7 + 7 + 15
     loss, g1, g2 = pl.pallas_call(
         kernel,
         out_shape=(
@@ -271,7 +295,17 @@
             collective_id=1, has_side_effects=True, vmem_limit_bytes=56 * 2**20
         ),
     )(one, two)
-    return loss[0, 0], g1, g2
+    loss, g1, g2 = pl.pallas_call(
+        finish_kernel,
+        out_shape=(
+            jax.ShapeDtypeStruct((1, 1), F32),
+            jax.ShapeDtypeStruct((B, B), F32),
+            jax.ShapeDtypeStruct((B, B), F32),
+        ),
+        in_specs=[vmem] * 5,
+        out_specs=(vmem,) * 3,
+    )(one, two, loss, g1, g2)
+    return loss.reshape(()), g1, g2
 
 
 def solution(mesh):

time: 63.1 us -> 55.1 us (0.87)
  Pallas kernels: 58.7 us -> 54.3 us
  local copies, waits for them, and re-layouts: 3.61 us -> 0 us
    pallas_call x1, Pallas kernels: 58.7 us -> 52.1 us  [step(): pl.pallas_call(kernel, out_shape=(jax.ShapeDtypeStruct((8, 128), F32), ja...]
    unnamed x4 -> x0, local copies, waits for them, and re-layouts: 2.42 us -> none
    pallas_call x0 -> x1, Pallas kernels: none -> 2.22 us  [step(): pl.pallas_call(finish_kernel, out_shape=(jax.ShapeDtypeStruct((1, 1), F32...]
    slice x1 -> x0, local copies, waits for them, and re-layouts: 1.19 us -> none  [step(): return (loss[0, 0], g1, g2)]
where the time goes in v2:
time: 55.1 us; the launch traced here: 55 us
  Pallas kernels  54.3 us (99%)
  between operations  0.64 us (1%)
    pallas_call x1, Pallas kernels, step(): pl.pallas_call(kernel, out_shape=(jax.ShapeDtypeStruct((8, 128), F32), ja...  52.1 us
    pallas_call x1, Pallas kernels, step(): pl.pallas_call(finish_kernel, out_shape=(jax.ShapeDtypeStruct((1, 1), F32...  2.22 us

profile of v2, /device:TPU:1, one launch (start us, length us, event | category | flops | bytes accessed | tf_op | source)
XLA Modules:
  0.0 55.0 jit_solution(15741366375608329408)
XLA Ops:
  0.6 52.1 %shard_map.49 = (f32[8,128]{1,0:T(8,128)}, f32[256,256]{1,0:T(8,128)}, f32[256,256]{1,0:T(8,128)}) custom-call(f32[256,256]{1,0:T(8,128)} %one_ref.3, f32[256,256]{1,0:T(8,128)} %two_ref.3), custom_call_target="tpu_custom_call" | custom-call | tf_op jit(solution)/shard_map/pallas_call | solution.py:273
  52.8 2.2 %shard_map.50 = (f32[1,1]{1,0:T(1,128)}, f32[256,256]{1,0:T(8,128)}, f32[256,256]{1,0:T(8,128)}) custom-call(f32[256,256]{1,0:T(8,128)} %one_ref.3, f32[256,256]{1,0:T(8,128)} %two_ref.3, f32[8,128]{1,0:T(8,128)} %get-tuple-element.9.loss_ref, f32[256,256]{1,0:T(8,128)} %get-tuple-element.10.g1_ref, f32[256,256]{1,0:T(8,128)} %get-tuple-element.11.g2_ref), custom_call_target="tpu_custom_call" | custom-call | tf_op jit(solution)/shard_map/pallas_call | solution.py:298

commit v3 on v2

--- a/solution.py
+++ b/solution.py
@@ -18,6 +18,9 @@
 NEAR = (4, 2, 1)
 HOP2 = ((2, 4), (1, 2), (4, 1))
 HOP3 = ((3, 4, 0, 96), (5, 2, 96, 80), (6, 1, 176, 80))
+FIRST = ((6, 4, 2), (3, 2, 1), (5, 1, 4))
+CORNER = ((3, 4, 0, 96), (5, 2, 96, 80), (6, 1, 176, 80))
+HALF = B // 2
 A, BB = 0, 1
 
 
@@ -73,9 +76,9 @@
     one_ref, two_ref, loss_ref, g1_ref, g2_ref,
     left, right, weights, t8,
     tmine, tsib, tpair, tall,
-    nsib_out, nsib_in, n_out, n_in, n_own,
-    c_out, c_in, c_own,
-    l_pair_out, l_pair_in, l_a_out, l_a_in, l_b_out, l_b_in,
+    nsib_out, nsib_in, n_out, n_mid, n_corner, n_last, n_acc,
+    c_out, c_mid, c_corner, c_last, c_acc,
+    recip_ref, l_out, l_in,
     ss, rs,
 ):
     counter = [0]
@@ -146,18 +149,21 @@
             got[group, frm].wait_recv()
             last[group, via] = send(block(group, frm, first, n), block(group, 7, first, n), peer(group, via))
         side[frm] = to_sibling(frm)
+    score(0, 8, 4, 7)
     for frm, *_ in HOP3:
         side[frm].wait_recv()
     score(8, 14, 0, 7)
-    score(0, 8, 4, 7)
     for copy in last.values():
         copy.wait_recv()
     side[7] = to_sibling(7)
     score(0, 14, 7, 8)
     side[7].wait_recv()
     score(14, 16, 0, 8)
-
-    tmine[...] = jnp.sum(t8[...], axis=0, keepdims=True)
+    unit_l, unit_r = left[rows(0), :].astype(F32), right[rows(0), :].astype(F32)
+    dots = jnp.sum(jnp.sum(unit_l * unit_r, axis=1, keepdims=True), axis=0, keepdims=True)
+    for p in range(16):
+        tmine[p : p + 1, :] = jnp.sum(t8[:, rows(p)], axis=0, keepdims=True)
+    tmine[16:24, :] = jnp.broadcast_to(dots, (8, B))
     pair = send(tmine, tsib, sibling())
 
     def numer(places, core):
@@ -174,83 +180,99 @@
         arrival.wait_recv()
         for p, part in zip(places, parts):
             part = part + nsib_in[p].astype(F32)
-            if p == 0:
-                n_own[...] = part
+            if p < 4:
+                n_acc[p] = part
             else:
                 n_out[p] = part.astype(BF16)
-        for p in reversed(places):
-            if p:
-                ncopies[p] = send(n_out.at[p], n_in.at[ORDER[p]], peer(A, ORDER[p]))
 
     def column(places):
         span = rows(places[0], len(places))
-        part = nn(weights[span, :] * recip_row, left[...])
+        part = nn(weights[span, :] * recip_ref[...].astype(BF16), left[...])
         for n, p in enumerate(places):
-            if p == 0:
-                c_own[...] = part[:B]
+            if p < 4:
+                c_acc[p] = part[n * B : n * B + B]
             else:
                 c_out[p] = part[n * B : n * B + B].astype(BF16)
-        for p in reversed(places):
-            if p:
-                ccopies[p] = send(c_out.at[p], c_in.at[ORDER[p]], peer(BB, ORDER[p]))
-
-    ncopies, ccopies = {}, {}
+
+    def first_stage(group, out, mid, corner):
+        copies = {}
+        for k, _, first, n in CORNER:
+            span = pl.ds(first, n)
+            copies[k] = send(out.at[PLACE[7], span], corner.at[span], peer(group, k))
+        for h in range(2):
+            span = pl.ds(h * HALF, HALF)
+            for k, via, to in FIRST:
+                copies[to, h] = send(out.at[PLACE[k], span], mid.at[PLACE[to], span], peer(group, via))
+        return copies
+
+    def second_stage(group, copies, acc, out, mid, corner, last):
+        done = {}
+        for k, to, first, n in CORNER:
+            copies[k].wait_recv()
+            span = pl.ds(first, n)
+            acc[PLACE[to], span] += corner[span].astype(F32)
+        for h in range(2):
+            span = pl.ds(h * HALF, HALF)
+            for _, _, to in FIRST:
+                copies[to, h].wait_recv()
+            for _, _, to in FIRST:
+                p = PLACE[to]
+                out[p, span] = (acc[p, span] + mid[p, span].astype(F32)).astype(BF16)
+                done[to, h] = send(out.at[p, span], last.at[p, span], peer(group, to))
+        return done
+
+    def whole(copies, acc, last):
+        for copy in copies.values():
+            copy.wait_recv()
+        return (acc[0] + last[1].astype(F32)) + (last[2].astype(F32) + last[3].astype(F32))
+
     near, far = (0, 1, 2, 3), (4, 5, 6, 7)
     far_sib = for_sibling(far)
     pair.wait_recv()
-    other = tsib[...]
-    tpair[...] = tmine[...] + jnp.concatenate(
-        [other[:, (p ^ 1) * B : (p ^ 1) * B + B] for p in range(16)], axis=1
-    )
+    for p in range(16):
+        tpair[p : p + 1, :] = tmine[p : p + 1, :] + tsib[(p ^ 1) : (p ^ 1) + 1, :]
+    tpair[16:24, :] = tmine[16:24, :] + tsib[16:24, :]
     tcopies = [send(tpair, tall.at[k], peer(A, k)) for k in FAR]
     near_sib = for_sibling(near)
     for_members(far, far_sib)
+    n_copies = first_stage(A, n_out, n_mid, n_corner)
     for copy in tcopies:
         copy.wait_recv()
 
-    def their_totals(k):
-        if k == 0:
-            return tpair[...]
-        theirs = tall[k]
-        places = [2 * PLACE[m ^ k] + c for m in ORDER for c in (0, 1)]
-        return jnp.concatenate([theirs[:, p * B : p * B + B] for p in places], axis=1)
-
-    totals = tree({k: their_totals(k) for k in range(8)})
-    recip = 1.0 / totals
-    recip_row = recip.astype(BF16)
+    def total_row(m, c):
+        parts = {}
+        for k in range(8):
+            p = 2 * PLACE[m ^ k] + c
+            parts[k] = tall[k, p : p + 1, :] if k else tpair[p : p + 1, :]
+        return tree(parts)
+
+    logs = {}
+    for m in range(8):
+        both = [total_row(m, c) for c in range(2)]
+        for c in range(2):
+            recip_ref[:, rows(2 * PLACE[m] + c)] = 1.0 / both[c]
+        logs[m] = jnp.log(both[0]) + jnp.log(both[1])
+    diagonals = tree({k: tall[k, 16:17, :] if k else tpair[16:17, :] for k in range(8)})
+    cube = jnp.sum(tree(logs), axis=1, keepdims=True) - diagonals[:, :1] * SHARP
+    l_out[...] = jnp.broadcast_to(cube, (8, 128))
+    lcopies = [send(l_out, l_in.at[k], peer(BB, k)) for k in FAR]
 
     column(far)
+    c_copies = first_stage(BB, c_out, c_mid, c_corner)
     for_members(near, near_sib)
     column(near)
-
-    mine = jnp.sum(jnp.log(totals[:, :B]), axis=1, keepdims=True)
-    unit_l, unit_r = left[rows(0), :].astype(F32), right[rows(0), :].astype(F32)
-    dots = jnp.sum(jnp.sum(unit_l * unit_r, axis=1, keepdims=True), axis=0, keepdims=True)
-    l_pair_out[...] = jnp.broadcast_to(mine - dots * SHARP, (8, 128))
-    copy = send(l_pair_out, l_pair_in, sibling())
-    copy.wait_recv()
-    l_a_out[...] = l_pair_out[...] + l_pair_in[...]
-    copies = [send(l_a_out, l_a_in.at[k], peer(A, k)) for k in FAR]
-    for copy in copies:
+    n_copies = second_stage(A, n_copies, n_acc, n_out, n_mid, n_corner, n_last)
+    c_copies = second_stage(BB, c_copies, c_acc, c_out, c_mid, c_corner, c_last)
+
+    scale = jnp.transpose(jnp.broadcast_to(recip_ref[:, :B], (128, B)))
+    scale = jnp.concatenate([scale, scale], axis=1)
+    total = whole(n_copies, n_acc, n_last)
+    g1_ref[...] = (total * scale - right[rows(0), :].astype(F32)) * SHARP
+    total = whole(c_copies, c_acc, c_last)
+    g2_ref[...] = (total - left[rows(0), :].astype(F32)) * SHARP
+    for copy in lcopies:
         copy.wait_recv()
-    l_b_out[...] = tree({k: l_a_in[k] if k else l_a_out[...] for k in range(8)})
-    copies = [send(l_b_out, l_b_in.at[k], peer(BB, k)) for k in FAR]
-    for copy in copies:
-        copy.wait_recv()
-    loss_ref[...] = tree({k: l_b_in[k] if k else l_b_out[...] for k in range(8)}) * (1.0 / (128 * B))
-
-    scale = jnp.transpose(jnp.broadcast_to(recip[:, :B], (128, B)))
-    scale = jnp.concatenate([scale, scale], axis=1)
-    total = n_own[...]
-    for p in reversed(range(1, 8)):
-        ncopies[p].wait_recv()
-        total = total + n_in[ORDER[p]].astype(F32)
-    g1_ref[...] = (total * scale - right[rows(0), :].astype(F32)) * SHARP
-    total = c_own[...]
-    for p in reversed(range(1, 8)):
-        ccopies[p].wait_recv()
-        total = total + c_in[ORDER[p]].astype(F32)
-    g2_ref[...] = (total - left[rows(0), :].astype(F32)) * SHARP
+    loss_ref[...] = tree({k: l_in[k] if k else l_out[...] for k in range(8)}) * (1.0 / (128 * B))
     for copy in started:
         copy.wait_send()
 
@@ -265,11 +287,12 @@
 
 def step(one, two):
     vmem = pl.BlockSpec(memory_space=pltpu.VMEM)
-    blocks = pltpu.VMEM((8, B, B), BF16)
+    blocks = lambda n: pltpu.VMEM((n, B, B), BF16)
+    parts = [blocks(8), blocks(4), pltpu.VMEM((B, B), BF16), blocks(4), pltpu.VMEM((4, B, B), F32)]
     tile = pltpu.VMEM((8, 128), F32)
     tiles = pltpu.VMEM((8, 8, 128), F32)
-    row = pltpu.VMEM((1, 16 * B), F32)
-    copies = 2 * 9 + 8 + 8 + 2 + 7 + 7 + 15
+    table = pltpu.VMEM((24, B), F32)
+    copies = 2 * 9 + 8 + 8 + 2 + 7 + 2 * 15
     loss, g1, g2 = pl.pallas_call(
         kernel,
         out_shape=(
@@ -284,10 +307,9 @@
             pltpu.VMEM((8 * B, B), BF16),
             pltpu.VMEM((8 * B, 16 * B), BF16),
             pltpu.VMEM((8, 16 * B), F32),
-            row, row, row, pltpu.VMEM((8, 1, 16 * B), F32),
-            blocks, blocks, blocks, blocks, pltpu.VMEM((B, B), F32),
-            blocks, blocks, pltpu.VMEM((B, B), F32),
-            tile, tile, tile, tiles, tile, tiles,
+            table, table, table, pltpu.VMEM((8, 24, B), F32),
+            blocks(8), blocks(8), *parts, *parts,
+            pltpu.VMEM((1, 16 * B), F32), tile, tiles,
             pltpu.SemaphoreType.DMA((copies,)),
             pltpu.SemaphoreType.DMA((copies,)),
         ],

time: 55.1 us -> 51.2 us (0.929)
  Pallas kernels: 54.3 us -> 50.4 us
    pallas_call x1, Pallas kernels: 52.1 us -> 48.2 us  [step(): pl.pallas_call(kernel, out_shape=(jax.ShapeDtypeStruct((8, 128), F32), ja...]
where the time goes in v3:
time: 51.2 us; the launch traced here: 51.1 us
  Pallas kernels  50.4 us (98%)
  between operations  0.64 us (1%)
    pallas_call x1, Pallas kernels, step(): pl.pallas_call(kernel, out_shape=(jax.ShapeDtypeStruct((8, 128), F32), ja...  48.2 us
    pallas_call x1, Pallas kernels, step(): pl.pallas_call(finish_kernel, out_shape=(jax.ShapeDtypeStruct((1, 1), F32...  2.22 us

profile of v3, /device:TPU:1, one launch (start us, length us, event | category | flops | bytes accessed | tf_op | source)
XLA Modules:
  0.0 51.1 jit_solution(4876794999951947624)
XLA Ops:
  0.6 48.2 %shard_map.49 = (f32[8,128]{1,0:T(8,128)}, f32[256,256]{1,0:T(8,128)}, f32[256,256]{1,0:T(8,128)}) custom-call(f32[256,256]{1,0:T(8,128)} %one_ref.3, f32[256,256]{1,0:T(8,128)} %two_ref.3), custom_call_target="tpu_custom_call" | custom-call | tf_op jit(solution)/shard_map/pallas_call | solution.py:296
  48.8 2.2 %shard_map.50 = (f32[1,1]{1,0:T(1,128)}, f32[256,256]{1,0:T(8,128)}, f32[256,256]{1,0:T(8,128)}) custom-call(f32[256,256]{1,0:T(8,128)} %one_ref.3, f32[256,256]{1,0:T(8,128)} %two_ref.3, f32[8,128]{1,0:T(8,128)} %get-tuple-element.9.loss_ref, f32[256,256]{1,0:T(8,128)} %get-tuple-element.10.g1_ref, f32[256,256]{1,0:T(8,128)} %get-tuple-element.11.g2_ref), custom_call_target="tpu_custom_call" | custom-call | tf_op jit(solution)/shard_map/pallas_call | solution.py:320

commit v4 on v3

--- a/solution.py
+++ b/solution.py
@@ -21,6 +21,7 @@
 FIRST = ((6, 4, 2), (3, 2, 1), (5, 1, 4))
 CORNER = ((3, 4, 0, 96), (5, 2, 96, 80), (6, 1, 176, 80))
 HALF = B // 2
+EXTRA = pl.ds(16 * B, 128)
 A, BB = 0, 1
 
 
@@ -101,11 +102,12 @@
         for group in (A, BB):
             pl.semaphore_signal(barrier, 1, device_id=peer(group, k), device_id_type=MESH)
 
-    one, two = one_ref[...], two_ref[...]
-    norm_one = jnp.sqrt(jnp.sum(one * one, axis=1, keepdims=True))
-    norm_two = jnp.sqrt(jnp.sum(two * two, axis=1, keepdims=True))
-    left[rows(0), :] = (one / norm_one).astype(BF16)
-    right[rows(0), :] = (two / norm_two).astype(BF16)
+    def unit_rows(ref):
+        x = ref[...]
+        return (x / jnp.sqrt(jnp.sum(x * x, axis=1, keepdims=True))).astype(BF16)
+
+    right[rows(0), :] = unit_rows(two_ref)
+    left[rows(0), :] = unit_rows(one_ref)
     pl.semaphore_wait(barrier, 7)
 
     bufs = (left, right)
@@ -119,8 +121,9 @@
 
     got, side = {}, {}
     for d in NEAR:
-        for group in (BB, A):
-            got[group, d] = send(block(group, 0), block(group, d), peer(group, d))
+        got[BB, d] = send(block(BB, 0), block(BB, d), peer(BB, d))
+    for d in NEAR:
+        got[A, d] = send(block(A, 0), block(A, d), peer(A, d))
     side[0] = to_sibling(0)
     for frm, via in HOP2:
         for group in (BB, A):
@@ -162,8 +165,8 @@
     unit_l, unit_r = left[rows(0), :].astype(F32), right[rows(0), :].astype(F32)
     dots = jnp.sum(jnp.sum(unit_l * unit_r, axis=1, keepdims=True), axis=0, keepdims=True)
     for p in range(16):
-        tmine[p : p + 1, :] = jnp.sum(t8[:, rows(p)], axis=0, keepdims=True)
-    tmine[16:24, :] = jnp.broadcast_to(dots, (8, B))
+        tmine[:, rows(p)] = jnp.sum(t8[:, rows(p)], axis=0, keepdims=True)
+    tmine[:, EXTRA] = jnp.broadcast_to(dots, (1, 128))
     pair = send(tmine, tsib, sibling())
 
     def numer(places, core):
@@ -186,23 +189,24 @@
                 n_out[p] = part.astype(BF16)
 
     def column(places):
-        span = rows(places[0], len(places))
-        part = nn(weights[span, :] * recip_ref[...].astype(BF16), left[...])
-        for n, p in enumerate(places):
+        scale = recip_ref[...].astype(BF16)
+        for p in places:
+            part = nn(weights[rows(p), :] * scale, left[...])
             if p < 4:
-                c_acc[p] = part[n * B : n * B + B]
+                c_acc[p] = part
             else:
-                c_out[p] = part[n * B : n * B + B].astype(BF16)
-
-    def first_stage(group, out, mid, corner):
+                c_out[p] = part.astype(BF16)
+
+    def first_stage(group, out, mid, corner, members):
         copies = {}
-        for k, _, first, n in CORNER:
+        for k, _, first, n in CORNER if 7 in members else ():
             span = pl.ds(first, n)
             copies[k] = send(out.at[PLACE[7], span], corner.at[span], peer(group, k))
         for h in range(2):
             span = pl.ds(h * HALF, HALF)
             for k, via, to in FIRST:
-                copies[to, h] = send(out.at[PLACE[k], span], mid.at[PLACE[to], span], peer(group, via))
+                if k in members:
+                    copies[to, h] = send(out.at[PLACE[k], span], mid.at[PLACE[to], span], peer(group, via))
         return copies
 
     def second_stage(group, copies, acc, out, mid, corner, last):
@@ -230,12 +234,12 @@
     far_sib = for_sibling(far)
     pair.wait_recv()
     for p in range(16):
-        tpair[p : p + 1, :] = tmine[p : p + 1, :] + tsib[(p ^ 1) : (p ^ 1) + 1, :]
-    tpair[16:24, :] = tmine[16:24, :] + tsib[16:24, :]
+        tpair[:, rows(p)] = tmine[:, rows(p)] + tsib[:, rows(p ^ 1)]
+    tpair[:, EXTRA] = tmine[:, EXTRA] + tsib[:, EXTRA]
     tcopies = [send(tpair, tall.at[k], peer(A, k)) for k in FAR]
     near_sib = for_sibling(near)
     for_members(far, far_sib)
-    n_copies = first_stage(A, n_out, n_mid, n_corner)
+    n_copies = first_stage(A, n_out, n_mid, n_corner, FAR[:4])
     for copy in tcopies:
         copy.wait_recv()
 
@@ -243,7 +247,7 @@
         parts = {}
         for k in range(8):
             p = 2 * PLACE[m ^ k] + c
-            parts[k] = tall[k, p : p + 1, :] if k else tpair[p : p + 1, :]
+            parts[k] = tall[k, :, rows(p)] if k else tpair[:, rows(p)]
         return tree(parts)
 
     logs = {}
@@ -252,13 +256,15 @@
         for c in range(2):
             recip_ref[:, rows(2 * PLACE[m] + c)] = 1.0 / both[c]
         logs[m] = jnp.log(both[0]) + jnp.log(both[1])
-    diagonals = tree({k: tall[k, 16:17, :] if k else tpair[16:17, :] for k in range(8)})
+    diagonals = tree({k: tall[k, :, EXTRA] if k else tpair[:, EXTRA] for k in range(8)})
     cube = jnp.sum(tree(logs), axis=1, keepdims=True) - diagonals[:, :1] * SHARP
     l_out[...] = jnp.broadcast_to(cube, (8, 128))
     lcopies = [send(l_out, l_in.at[k], peer(BB, k)) for k in FAR]
 
-    column(far)
-    c_copies = first_stage(BB, c_out, c_mid, c_corner)
+    c_copies = {}
+    for places in ((7, 6), (5, 4)):
+        column(places)
+        c_copies |= first_stage(BB, c_out, c_mid, c_corner, [ORDER[p] for p in places])
     for_members(near, near_sib)
     column(near)
     n_copies = second_stage(A, n_copies, n_acc, n_out, n_mid, n_corner, n_last)
@@ -291,7 +297,7 @@
     parts = [blocks(8), blocks(4), pltpu.VMEM((B, B), BF16), blocks(4), pltpu.VMEM((4, B, B), F32)]
     tile = pltpu.VMEM((8, 128), F32)
     tiles = pltpu.VMEM((8, 8, 128), F32)
-    table = pltpu.VMEM((24, B), F32)
+    table = pltpu.VMEM((1, 16 * B + 128), F32)
     copies = 2 * 9 + 8 + 8 + 2 + 7 + 2 * 15
     loss, g1, g2 = pl.pallas_call(
         kernel,
@@ -307,7 +313,7 @@
             pltpu.VMEM((8 * B, B), BF16),
             pltpu.VMEM((8 * B, 16 * B), BF16),
             pltpu.VMEM((8, 16 * B), F32),
-            table, table, table, pltpu.VMEM((8, 24, B), F32),
+            table, table, table, pltpu.VMEM((8, 1, 16 * B + 128), F32),
             blocks(8), blocks(8), *parts, *parts,
             pltpu.VMEM((1, 16 * B), F32), tile, tiles,
             pltpu.SemaphoreType.DMA((copies,)),

time: 51.2 us -> 45.8 us (0.89)
  Pallas kernels: 50.4 us -> 45 us
    pallas_call x1, Pallas kernels: 48.2 us -> 42.8 us  [step(): pl.pallas_call(kernel, out_shape=(jax.ShapeDtypeStruct((8, 128), F32), ja...]
where the time goes in v4:
time: 45.8 us; the launch traced here: 45.6 us
  Pallas kernels  45 us (98%)
  between operations  0.64 us (1%)
    pallas_call x1, Pallas kernels, step(): pl.pallas_call(kernel, out_shape=(jax.ShapeDtypeStruct((8, 128), F32), ja...  42.8 us
    pallas_call x1, Pallas kernels, step(): pl.pallas_call(finish_kernel, out_shape=(jax.ShapeDtypeStruct((1, 1), F32...  2.22 us

profile of v4, /device:TPU:1, one launch (start us, length us, event | category | flops | bytes accessed | tf_op | source)
XLA Modules:
  0.0 45.6 jit_solution(7463028687343702760)
XLA Ops:
  0.6 42.8 %shard_map.49 = (f32[8,128]{1,0:T(8,128)}, f32[256,256]{1,0:T(8,128)}, f32[256,256]{1,0:T(8,128)}) custom-call(f32[256,256]{1,0:T(8,128)} %one_ref.3, f32[256,256]{1,0:T(8,128)} %two_ref.3), custom_call_target="tpu_custom_call" | custom-call | tf_op jit(solution)/shard_map/pallas_call | solution.py:302
  43.4 2.2 %shard_map.50 = (f32[1,1]{1,0:T(1,128)}, f32[256,256]{1,0:T(8,128)}, f32[256,256]{1,0:T(8,128)}) custom-call(f32[256,256]{1,0:T(8,128)} %one_ref.3, f32[256,256]{1,0:T(8,128)} %two_ref.3, f32[8,128]{1,0:T(8,128)} %get-tuple-element.9.loss_ref, f32[256,256]{1,0:T(8,128)} %get-tuple-element.10.g1_ref, f32[256,256]{1,0:T(8,128)} %get-tuple-element.11.g2_ref), custom_call_target="tpu_custom_call" | custom-call | tf_op jit(solution)/shard_map/pallas_call | solution.py:326

commit v5 on v4

--- a/solution.py
+++ b/solution.py
@@ -131,9 +131,9 @@
             got[group, frm | via] = send(block(group, frm), block(group, frm | via), peer(group, via))
         side[frm] = to_sibling(frm)
 
-    def score(l0, l1, j0, j1):
+    def score(blocks, j0, j1):
         n = (j1 - j0) * B
-        for lb in range(l0, l1):
+        for lb in blocks:
             lanes = rows(lb)
             w = jnp.exp2(nt(right[rows(j0, j1 - j0), :], left[lanes, :]) * EXP2_SCALE)
             part = jnp.sum(w.reshape(n // 8, 8, B), axis=0)
@@ -143,25 +143,28 @@
                 t8[:, lanes] += part
             weights[rows(j0, j1 - j0), lanes] = w.astype(BF16)
 
+    score((0, 2, 4, 6), 0, 4)
     for k in (0, *NEAR):
         side[k].wait_recv()
-    score(0, 8, 0, 4)
+    score((1, 3, 5, 7), 0, 4)
     last = {}
     for frm, via, first, n in HOP3:
         for group in (BB, A):
             got[group, frm].wait_recv()
             last[group, via] = send(block(group, frm, first, n), block(group, 7, first, n), peer(group, via))
         side[frm] = to_sibling(frm)
-    score(0, 8, 4, 7)
+    score(range(8), 4, 7)
+    score((8, 10, 12), 0, 7)
     for frm, *_ in HOP3:
         side[frm].wait_recv()
-    score(8, 14, 0, 7)
+    score((9, 11, 13), 0, 7)
     for copy in last.values():
         copy.wait_recv()
     side[7] = to_sibling(7)
-    score(0, 14, 7, 8)
+    score(range(14), 7, 8)
+    score((14,), 0, 8)
     side[7].wait_recv()
-    score(14, 16, 0, 8)
+    score((15,), 0, 8)
     unit_l, unit_r = left[rows(0), :].astype(F32), right[rows(0), :].astype(F32)
     dots = jnp.sum(jnp.sum(unit_l * unit_r, axis=1, keepdims=True), axis=0, keepdims=True)
     for p in range(16):
@@ -250,21 +253,21 @@
             parts[k] = tall[k, :, rows(p)] if k else tpair[:, rows(p)]
         return tree(parts)
 
-    logs = {}
+    totals = {}
     for m in range(8):
-        both = [total_row(m, c) for c in range(2)]
         for c in range(2):
-            recip_ref[:, rows(2 * PLACE[m] + c)] = 1.0 / both[c]
-        logs[m] = jnp.log(both[0]) + jnp.log(both[1])
-    diagonals = tree({k: tall[k, :, EXTRA] if k else tpair[:, EXTRA] for k in range(8)})
-    cube = jnp.sum(tree(logs), axis=1, keepdims=True) - diagonals[:, :1] * SHARP
-    l_out[...] = jnp.broadcast_to(cube, (8, 128))
-    lcopies = [send(l_out, l_in.at[k], peer(BB, k)) for k in FAR]
+            totals[m, c] = total_row(m, c)
+            recip_ref[:, rows(2 * PLACE[m] + c)] = 1.0 / totals[m, c]
 
     c_copies = {}
     for places in ((7, 6), (5, 4)):
         column(places)
         c_copies |= first_stage(BB, c_out, c_mid, c_corner, [ORDER[p] for p in places])
+    logs = tree({m: jnp.log(totals[m, 0]) + jnp.log(totals[m, 1]) for m in range(8)})
+    diagonals = tree({k: tall[k, :, EXTRA] if k else tpair[:, EXTRA] for k in range(8)})
+    cube = jnp.sum(logs, axis=1, keepdims=True) - diagonals[:, :1] * SHARP
+    l_out[...] = jnp.broadcast_to(cube, (8, 128))
+    lcopies = [send(l_out, l_in.at[k], peer(BB, k)) for k in FAR]
     for_members(near, near_sib)
     column(near)
     n_copies = second_stage(A, n_copies, n_acc, n_out, n_mid, n_corner, n_last)
@@ -272,10 +275,16 @@
 
     scale = jnp.transpose(jnp.broadcast_to(recip_ref[:, :B], (128, B)))
     scale = jnp.concatenate([scale, scale], axis=1)
+    def finish(ref, grad, out):
+        x = ref[...]
+        norm = jnp.sqrt(jnp.sum(x * x, axis=1, keepdims=True))
+        unit = x / norm
+        out[...] = (grad - unit * jnp.sum(unit * grad, axis=1, keepdims=True)) / norm
+
     total = whole(n_copies, n_acc, n_last)
-    g1_ref[...] = (total * scale - right[rows(0), :].astype(F32)) * SHARP
+    finish(one_ref, (total * scale - right[rows(0), :].astype(F32)) * SHARP, g1_ref)
     total = whole(c_copies, c_acc, c_last)
-    g2_ref[...] = (total - left[rows(0), :].astype(F32)) * SHARP
+    finish(two_ref, (total - left[rows(0), :].astype(F32)) * SHARP, g2_ref)
     for copy in lcopies:
         copy.wait_recv()
     loss_ref[...] = tree({k: l_in[k] if k else l_out[...] for k in range(8)}) * (1.0 / (128 * B))
@@ -283,12 +292,10 @@
         copy.wait_send()
 
 
-def finish_kernel(one_ref, two_ref, loss_ref, g1_ref, g2_ref, out_loss, out_one, out_two):
-    for x, grad, out in ((one_ref[...], g1_ref[...], out_one), (two_ref[...], g2_ref[...], out_two)):
-        norm = jnp.sqrt(jnp.sum(x * x, axis=1, keepdims=True))
-        unit = x / norm
-        out[...] = (grad - unit * jnp.sum(unit * grad, axis=1, keepdims=True)) / norm
+def hand_over(loss_ref, g1_ref, g2_ref, out_loss, out_one, out_two):
     out_loss[...] = loss_ref[0:1, 0:1]
+    out_one[...] = g1_ref[...]
+    out_two[...] = g2_ref[...]
 
 
 def step(one, two):
@@ -324,15 +331,15 @@
         ),
     )(one, two)
     loss, g1, g2 = pl.pallas_call(
-        finish_kernel,
+        hand_over,
         out_shape=(
             jax.ShapeDtypeStruct((1, 1), F32),
             jax.ShapeDtypeStruct((B, B), F32),
             jax.ShapeDtypeStruct((B, B), F32),
         ),
-        in_specs=[vmem] * 5,
+        in_specs=[vmem] * 3,
         out_specs=(vmem,) * 3,
-    )(one, two, loss, g1, g2)
+    )(loss, g1, g2)
     return loss.reshape(()), g1, g2
 
 

time: 45.8 us -> 45.2 us (0.987)
  Pallas kernels: 45 us -> 44.4 us
where the time goes in v5:
time: 45.2 us; the launch traced here: 45 us
  Pallas kernels  44.4 us (98%)
  between operations  0.64 us (1%)
    pallas_call x1, Pallas kernels, step(): pl.pallas_call(kernel, out_shape=(jax.ShapeDtypeStruct((8, 128), F32), ja...  42.5 us
    pallas_call x1, Pallas kernels, step(): pl.pallas_call(hand_over, out_shape=(jax.ShapeDtypeStruct((1, 1), F32), j...  1.85 us

profile of v5, /device:TPU:1, one launch (start us, length us, event | category | flops | bytes accessed | tf_op | source)
XLA Modules:
  0.0 45.0 jit_solution(9950435961883498543)
XLA Ops:
  0.6 42.5 %shard_map.49 = (f32[8,128]{1,0:T(8,128)}, f32[256,256]{1,0:T(8,128)}, f32[256,256]{1,0:T(8,128)}) custom-call(f32[256,256]{1,0:T(8,128)} %one_ref.1, f32[256,256]{1,0:T(8,128)} %two_ref.1), custom_call_target="tpu_custom_call" | custom-call | tf_op jit(solution)/shard_map/pallas_call | solution.py:309
  43.2 1.8 %shard_map.50 = (f32[1,1]{1,0:T(1,128)}, f32[256,256]{1,0:T(8,128)}, f32[256,256]{1,0:T(8,128)}) custom-call(f32[8,128]{1,0:T(8,128)} %get-tuple-element.9.loss_ref, f32[256,256]{1,0:T(8,128)} %get-tuple-element.10.g1_ref, f32[256,256]{1,0:T(8,128)} %get-tuple-element.11.g2_ref), custom_call_target="tpu_custom_call" | custom-call | tf_op jit(solution)/shard_map/pallas_call | solution.py:333

commit v6 on v5

--- a/solution.py
+++ b/solution.py
@@ -74,7 +74,8 @@
 
 
 def kernel(
-    one_ref, two_ref, loss_ref, g1_ref, g2_ref,
+    one_hbm, two_hbm, loss_ref, g1_ref, g2_ref,
+    one_ref, two_ref, in_sem,
     left, right, weights, t8,
     tmine, tsib, tpair, tall,
     nsib_out, nsib_in, n_out, n_mid, n_corner, n_last, n_acc,
@@ -96,6 +97,10 @@
         started.append(copy)
         return copy
 
+    load_two = pltpu.make_async_copy(two_hbm, two_ref, in_sem.at[0])
+    load_one = pltpu.make_async_copy(one_hbm, one_ref, in_sem.at[1])
+    load_two.start()
+    load_one.start()
     barrier = pltpu.get_barrier_semaphore()
     pl.semaphore_signal(barrier, 1, device_id=sibling(), device_id_type=MESH)
     for k in NEAR:
@@ -106,7 +111,9 @@
         x = ref[...]
         return (x / jnp.sqrt(jnp.sum(x * x, axis=1, keepdims=True))).astype(BF16)
 
+    load_two.wait()
     right[rows(0), :] = unit_rows(two_ref)
+    load_one.wait()
     left[rows(0), :] = unit_rows(one_ref)
     pl.semaphore_wait(barrier, 7)
 
@@ -121,15 +128,15 @@
 
     got, side = {}, {}
     for d in NEAR:
-        got[BB, d] = send(block(BB, 0), block(BB, d), peer(BB, d))
-    for d in NEAR:
-        got[A, d] = send(block(A, 0), block(A, d), peer(A, d))
+        for group in (A, BB):
+            got[group, d] = send(block(group, 0), block(group, d), peer(group, d))
     side[0] = to_sibling(0)
     for frm, via in HOP2:
-        for group in (BB, A):
+        for group in (A, BB):
             got[group, frm].wait_recv()
             got[group, frm | via] = send(block(group, frm), block(group, frm | via), peer(group, via))
-        side[frm] = to_sibling(frm)
+            if group == A:
+                side[frm] = to_sibling(frm)
 
     def score(blocks, j0, j1):
         n = (j1 - j0) * B
@@ -149,10 +156,11 @@
     score((1, 3, 5, 7), 0, 4)
     last = {}
     for frm, via, first, n in HOP3:
-        for group in (BB, A):
+        for group in (A, BB):
             got[group, frm].wait_recv()
             last[group, via] = send(block(group, frm, first, n), block(group, 7, first, n), peer(group, via))
-        side[frm] = to_sibling(frm)
+            if group == A:
+                side[frm] = to_sibling(frm)
     score(range(8), 4, 7)
     score((8, 10, 12), 0, 7)
     for frm, *_ in HOP3:
@@ -313,9 +321,12 @@
             jax.ShapeDtypeStruct((B, B), F32),
             jax.ShapeDtypeStruct((B, B), F32),
         ),
-        in_specs=[vmem] * 2,
+        in_specs=[pl.BlockSpec(memory_space=pltpu.HBM)] * 2,
         out_specs=(vmem,) * 3,
         scratch_shapes=[
+            pltpu.VMEM((B, B), F32),
+            pltpu.VMEM((B, B), F32),
+            pltpu.SemaphoreType.DMA((2,)),
             pltpu.VMEM((16 * B, B), BF16),
             pltpu.VMEM((8 * B, B), BF16),
             pltpu.VMEM((8 * B, 16 * B), BF16),

time: 45.2 us -> 44.9 us (level)
  no operation moved by 1% of the time
where the time goes in v6:
time: 44.9 us; the launch traced here: 44.7 us
  Pallas kernels  44.1 us (98%)
  between operations  0.64 us (1%)
    pallas_call x1, Pallas kernels, step(): pl.pallas_call(kernel, out_shape=(jax.ShapeDtypeStruct((8, 128), F32), ja...  42.3 us
    pallas_call x1, Pallas kernels, step(): pl.pallas_call(hand_over, out_shape=(jax.ShapeDtypeStruct((1, 1), F32), j...  1.85 us

profile of v6, /device:TPU:1, one launch (start us, length us, event | category | flops | bytes accessed | tf_op | source)
XLA Modules:
  0.0 44.7 jit_solution(9958443552055197936)
XLA Ops:
  0.6 42.3 %shard_map.49 = (f32[8,128]{1,0:T(8,128)}, f32[256,256]{1,0:T(8,128)}, f32[256,256]{1,0:T(8,128)}) custom-call(f32[256,256]{1,0:T(8,128)} %one_hbm.1, f32[256,256]{1,0:T(8,128)} %two_hbm.1), custom_call_target="tpu_custom_call" | custom-call | tf_op jit(solution)/shard_map/pallas_call | solution.py:317
  42.9 1.8 %shard_map.50 = (f32[1,1]{1,0:T(1,128)}, f32[256,256]{1,0:T(8,128)}, f32[256,256]{1,0:T(8,128)}) custom-call(f32[8,128]{1,0:T(8,128)} %get-tuple-element.9.loss_ref, f32[256,256]{1,0:T(8,128)} %get-tuple-element.10.g1_ref, f32[256,256]{1,0:T(8,128)} %get-tuple-element.11.g2_ref), custom_call_target="tpu_custom_call" | custom-call | tf_op jit(solution)/shard_map/pallas_call | solution.py:344
